TPU v7x, 256 devices: a whole 4x4x8 slice. The times are simulated.
256 devices in a mesh: dp: 8 (over z), expert: 32 (over x, y, core).
Axes of the slice: x: 4, y: 4, z: 8, core: 2. Of those that a mesh axis runs over, the one named last changes fastest.
Arguments:
- tokens: bfloat16 [2048, 7168], P('expert', 'dp'), may hold values from -6 to 6
- tangent: bfloat16 [2048, 7168], P('expert', 'dp'), may hold values from -6 to 6
- cotangent: bfloat16 [2048, 7168], P('expert', 'dp'), may hold values from -3 to 3
- routing: int32 [2048, 8], P('expert'), may hold values from 0 to 31, all different within a row; in each aligned block of 64 rows (0 to 63, 64 to 127, ...) at most 18 rows name the same one
- gate_weights: float32 [2048, 8], P('expert'), may hold values from 0.1 to 0.6
- gate_proj: bfloat16 [32, 7168, 2048], P('expert', 'dp'), may hold values from -0.0625 to 0.0625
- up_proj: bfloat16 [32, 7168, 2048], P('expert', 'dp'), may hold values from -0.0625 to 0.0625
- down_proj: bfloat16 [32, 2048, 7168], P('expert', None, 'dp'), may hold values from -0.125 to 0.125
Outputs:
- hessian_product: float32 [2048, 7168], P('expert', 'dp')
Inputs may be any that keep to these rules, and one draw needn't show every extreme that they name: `routing`: each token names 8 different experts. In each aligned block of 64 tokens (the tokens of one index of expert) no expert is named more than 18 times, a bound that some block reaches.
All inputs are finite; a program needn't handle non-finite values.
Results may differ from a plain program's by a relative error of at most 0.0041.
Values may be sent and summed in bfloat16 or wider, within the bound.
A program may use at most 128 MiB of HBM per device.

v0:
```python
import jax
import jax.numpy as jnp
from jax import lax
from jax.sharding import PartitionSpec as P

TOP = 8


def second_order(pre_gate, pre_up, tangent_gate, tangent_up, back_hidden):
    sigma = jax.nn.sigmoid(pre_gate)
    first_slope = sigma * (1.0 + pre_gate * (1.0 - sigma))
    second_slope = sigma * (1.0 - sigma) * (2.0 + pre_gate * (1.0 - 2.0 * sigma))
    factor_a = back_hidden * (second_slope * tangent_gate * pre_up + first_slope * tangent_up)
    factor_b = back_hidden * first_slope * tangent_gate
    return (factor_a.astype(jnp.bfloat16), factor_b.astype(jnp.bfloat16))


def contract_last(left_rows, right_matrix):
    return lax.dot_general(
        left_rows, right_matrix, (((1,), (1,)), ((), ())), preferred_element_type=jnp.float32
    )


def shards(tokens, tangent, cotangent, routing, gate_weights, gate_proj, up_proj, down_proj):
    expert_count = lax.axis_size("expert")
    tok_rows = tokens.shape[0]
    feat_cols = tokens.shape[1]
    capacity = min(tok_rows, tok_rows * TOP // expert_count * 9 // 8)
    slot_total = expert_count * capacity
    routed_flat = routing.reshape(-1)
    route_hits = (
        routed_flat[:, None] == jnp.arange(expert_count, dtype=jnp.int32)[None, :]
    ).astype(jnp.int32)
    slot_index = jnp.sum((jnp.cumsum(route_hits, axis=0) - route_hits) * route_hits, axis=1)
    target_row = routed_flat * capacity + slot_index

    def scatter_rows(values):
        spread = jnp.repeat(values, TOP, axis=0)
        zero_buf = jnp.zeros((slot_total, values.shape[1]), values.dtype)
        return zero_buf.at[target_row].set(spread).reshape(expert_count, capacity, values.shape[1])

    x_rows = lax.all_to_all(
        scatter_rows(tokens), "expert", split_axis=0, concat_axis=0, tiled=True
    ).reshape(slot_total, feat_cols)
    paired = jnp.concatenate([tangent, cotangent], axis=1)
    paired_rows = lax.all_to_all(
        scatter_rows(paired), "expert", split_axis=0, concat_axis=0, tiled=True
    ).reshape(slot_total, 2 * feat_cols)
    v_rows = paired_rows[:, :feat_cols]
    c_rows = paired_rows[:, feat_cols:]
    gate_cols = gate_proj[0]
    up_cols = up_proj[0]
    down_rows = down_proj[0]
    part_gate = jnp.dot(x_rows, gate_cols, preferred_element_type=jnp.float32)
    part_up = jnp.dot(x_rows, up_cols, preferred_element_type=jnp.float32)
    part_tgate = jnp.dot(v_rows, gate_cols, preferred_element_type=jnp.float32)
    part_tup = jnp.dot(v_rows, up_cols, preferred_element_type=jnp.float32)
    part_back = contract_last(c_rows, down_rows)
    summed = (
        lax.psum_scatter(part_gate, "dp", scatter_dimension=0, tiled=True),
        lax.psum_scatter(part_up, "dp", scatter_dimension=0, tiled=True),
        lax.psum_scatter(part_tgate, "dp", scatter_dimension=0, tiled=True),
        lax.psum_scatter(part_tup, "dp", scatter_dimension=0, tiled=True),
        lax.psum_scatter(part_back, "dp", scatter_dimension=0, tiled=True),
    )
    factor_a, factor_b = second_order(summed[0], summed[1], summed[2], summed[3], summed[4])
    factors = jnp.stack([factor_a, factor_b])
    piece = lax.all_gather(factors, "dp", axis=1, tiled=True)
    result_rows = contract_last(piece[0], gate_cols) + contract_last(piece[1], up_cols)
    outgoing = result_rows.astype(jnp.bfloat16).reshape(expert_count, capacity, feat_cols)
    returned = lax.all_to_all(outgoing, "expert", split_axis=0, concat_axis=0, tiled=True).reshape(
        slot_total, feat_cols
    )
    gathered = returned[target_row].reshape(tok_rows, TOP, feat_cols).astype(jnp.float32)
    return jnp.sum(gate_weights[:, :, None] * gathered, axis=1)


def solution(mesh):
    in_specs = (
        P("expert", "dp"),
        P("expert", "dp"),
        P("expert", "dp"),
        P("expert", None),
        P("expert", None),
        P("expert", "dp", None),
        P("expert", "dp", None),
        P("expert", None, "dp"),
    )
    out_specs = P("expert", "dp")
    return jax.shard_map(shards, mesh=mesh, in_specs=in_specs, out_specs=out_specs, check_vma=False)
```

profile of v0, /device:TPU:1, one launch (start us, length us, event | category | flops | bytes accessed | tf_op | source)
XLA Modules:
  0.0 463.8 jit_solution(245255507557251218)
XLA Ops:
  10.0 3.0 scatter_custom_fusion.1
  13.3 29.3 %all_to_all.15 = bf16[32,18,896]{2,1,0:T(8,128)(2,1)S(1)} all-to-all(bf16[32,18,896]{2,1,0:T(8,128)(2,1)S(1)} %reshape.79), channel_id=1, replica_groups=mesh['dp'=8,'expert'=32] {'expert'}, dimensions={0} | all-to-all | bytes 2064384 | tf_op jit(solution)/shard_map/all_to_all | solution.py:42
  42.9 6.3 %fusion.4 = f32[576,2048]{1,0:T(8,128)} fusion(bf16[576,896]{1,0:T(8,128)(2,1)S(1)} %reshape.80, bf16[1,896,2048]{2,1,0:T(8,128)(2,1)} %param.14), kind=kOutput, calls=%fused_computation.7 | convolution fusion | flops 2113929216 | bytes 9420800 | tf_op jit(solution)/shard_map/dot_general | solution.py:55
  49.3 6.3 %fusion.10 = f32[576,2048]{1,0:T(8,128)} fusion(bf16[576,896]{1,0:T(8,128)(2,1)S(1)} %reshape.80, bf16[1,896,2048]{2,1,0:T(8,128)(2,1)} %param.13), kind=kOutput, calls=%fused_computation.13 | convolution fusion | flops 2113929216 | bytes 9420800 | tf_op jit(solution)/shard_map/dot_general | solution.py:54
  56.6 4.8 %scatter_custom_fusion = bf16[576,1792]{1,0:T(8,128)(2,1)} fusion(s32[512]{0:T(512)S(1)} %bitcast.64, bf16[]{:T(256)} %constant.7.clone.1, bf16[64,1792]{1,0:T(8,128)(2,1)S(1)} %pad_maximum_fusion.1), kind=kCustom, calls=%fused_computation.22 | custom fusion | bytes 2293762 | tf_op jit(solution)/shard_map/scatter | solution.py:40
  61.4 2.6 reshape.76
  64.0 39.1 %all_to_all.16 = bf16[32,18,1792]{2,1,0:T(8,128)(2,1)} all-to-all(bf16[32,18,1792]{2,1,0:T(8,128)(2,1)S(1)} %reshape.76), channel_id=1, replica_groups=mesh['dp'=8,'expert'=32] {'expert'}, dimensions={0} | all-to-all | bytes 4128768 | tf_op jit(solution)/shard_map/all_to_all | solution.py:46
  103.1 2.8 reshape.77
  105.9 6.4 %fusion.8 = f32[576,2048]{1,0:T(8,128)} fusion(bf16[1,896,2048]{2,1,0:T(8,128)(2,1)} %param.13, bf16[576,1792]{1,0:T(8,128)(2,1)S(1)} %reshape.77), kind=kOutput, calls=%fused_computation.11 | convolution fusion | flops 2113929216 | bytes 9420800 | tf_op jit(solution)/shard_map/dot_general | solution.py:56
  112.6 6.3 %fusion.2 = f32[576,2048]{1,0:T(8,128)} fusion(bf16[1,896,2048]{2,1,0:T(8,128)(2,1)} %param.14, bf16[576,1792]{1,0:T(8,128)(2,1)S(1)} %reshape.77), kind=kOutput, calls=%fused_computation.5 | convolution fusion | flops 2113929216 | bytes 9420800 | tf_op jit(solution)/shard_map/dot_general | solution.py:57
  118.9 6.4 %fusion.12 = f32[576,2048]{1,0:T(8,128)} fusion(bf16[1,2048,896]{2,1,0:T(8,128)(2,1)} %param.15, bf16[576,1792]{1,0:T(8,128)(2,1)S(1)} %reshape.77), kind=kOutput, calls=%fused_computation.15 | convolution fusion | flops 2113929216 | bytes 9420800 | tf_op jit(solution)/shard_map/dot_general | solution.py:19
  125.4 44.6 %reduce-scatter.8.cloned.1.call-done = f32[72,2048]{1,0:T(8,128)} async-done(((f32[576,2048]{1,0:T(8,128)}), f32[72,2048]{1,0:T(8,128)}) %reduce-scatter.8.cloned.1.call-update) | async-done | bytes 589840 | tf_op jit(solution)/shard_map/reduce_scatter | solution.py:60
  170.0 61.5 %reduce-scatter.10.cloned.1.call-done = f32[72,2048]{1,0:T(8,128)} async-done(((f32[576,2048]{1,0:T(8,128)}), f32[72,2048]{1,0:T(8,128)}) %reduce-scatter.10.cloned.1.call-update) | async-done | bytes 589840 | tf_op jit(solution)/shard_map/reduce_scatter | solution.py:62
  231.5 61.3 %reduce-scatter.14.cloned.1.call-done = f32[72,2048]{1,0:T(8,128)} async-done(((f32[576,2048]{1,0:T(8,128)}), f32[72,2048]{1,0:T(8,128)}) %reduce-scatter.14.cloned.1.call-update) | async-done | bytes 589840 | tf_op jit(solution)/shard_map/reduce_scatter | solution.py:63
  292.8 61.3 %reduce-scatter.6.cloned.1.call-done = f32[72,2048]{1,0:T(8,128)} async-done(((f32[576,2048]{1,0:T(8,128)}), f32[72,2048]{1,0:T(8,128)}) %reduce-scatter.6.cloned.1.call-update) | async-done | bytes 589840 | tf_op jit(solution)/shard_map/reduce_scatter | solution.py:64
  354.1 2.2 fusion.37
  357.2 58.5 %all-gather.2.cloned.1.call-done = bf16[2,576,2048]{2,1,0:T(8,128)(2,1)} async-done(((bf16[2,72,2048]{2,1,0:T(8,128)(2,1)}), bf16[2,576,2048]{2,1,0:T(8,128)(2,1)}) %all-gather.2.cloned.1.call-update) | async-done | bytes 4718608 | tf_op jit(solution)/shard_map/all_gather | solution.py:68
  415.7 5.5 %fusion = f32[576,896]{1,0:T(8,128)S(1)} fusion(bf16[1,896,2048]{2,1,0:T(8,128)(2,1)} %param.14, bf16[2,576,2048]{2,1,0:T(8,128)(2,1)} %all-gather.2.cloned.1.call-done), kind=kOutput, calls=%fused_computation.3 | convolution fusion | flops 2113929216 | bytes 8093696 | tf_op jit(solution)/shard_map/dot_general | solution.py:19
  421.3 2.7 add_convert_fusion
  423.9 1.3 reshape.81
  425.2 7.5 %all-to-all-start.2 = ((bf16[32,18,896]{2,1,0:T(8,128)(2,1)}), bf16[32,18,896]{2,1,0:T(8,128)(2,1)S(1)}, u32[]{:S(2)}, u32[]{:S(2)}) async-start(bf16[32,18,896]{2,1,0:T(8,128)(2,1)} %reshape.81), calls=%async_computation.7 | async-start | bytes 2752512 | tf_op jit(solution)/shard_map/all_to_all | solution.py:71
  432.8 20.4 %all-to-all-done.2 = bf16[32,18,896]{2,1,0:T(8,128)(2,1)S(1)} async-done(((bf16[32,18,896]{2,1,0:T(8,128)(2,1)}), bf16[32,18,896]{2,1,0:T(8,128)(2,1)S(1)}, u32[]{:S(2)}, u32[]{:S(2)}) %all-to-all-start.2) | async-done | bytes 1032224 | tf_op jit(solution)/shard_map/all_to_all | solution.py:71
  453.6 2.1 gather_fusion
  455.6 1.3 fusion.14
  (45 shorter events, 6.8 us)
Async XLA Ops:
  6.5 3.4 copy-start
  6.5 118.8 %reduce-scatter.12.cloned.1.call-start = ((), (), s32[]{:S(2)}) async-start(), calls=%async_computation.11 | async-start | bytes 5308416 | tf_op jit(solution)/shard_map/reduce_scatter | solution.py:61
  49.2 120.8 %reduce-scatter.8.cloned.1.call-start = ((), (), s32[]{:S(2)}) async-start(), calls=%async_computation.9 | async-start | bytes 5308416 | tf_op jit(solution)/shard_map/reduce_scatter | solution.py:60
  55.6 0.9 copy-start.1
  55.6 1.0 copy-start.2
  55.6 175.8 %reduce-scatter.10.cloned.1.call-start = ((), (), s32[]{:S(2)}) async-start(), calls=%async_computation.10 | async-start | bytes 5308416 | tf_op jit(solution)/shard_map/reduce_scatter | solution.py:62
  112.3 180.5 %reduce-scatter.14.cloned.1.call-start = ((), (), s32[]{:S(2)}) async-start(), calls=%async_computation.12 | async-start | bytes 5308416 | tf_op jit(solution)/shard_map/reduce_scatter | solution.py:63
  118.9 235.2 %reduce-scatter.6.cloned.1.call-start = ((), (), s32[]{:S(2)}) async-start(), calls=%async_computation.8 | async-start | bytes 5308416 | tf_op jit(solution)/shard_map/reduce_scatter | solution.py:64
  125.3 290.4 %all-gather.2.cloned.1.call-start = ((), (), s32[]{:S(2)}) async-start(), calls=%async_computation.13 | async-start | bytes 5308416 | tf_op jit(solution)/shard_map/all_gather | solution.py:68
  415.7 5.5 %copy-start.4 = (bf16[2,576,2048]{2,1,0:T(8,128)(2,1)S(1)}, bf16[2,576,2048]{2,1,0:T(8,128)(2,1)}, u32[]{:S(2)}) copy-start(bf16[2,576,2048]{2,1,0:T(8,128)(2,1)} %all-gather.2.cloned.1.call-done) | copy-start | bytes 14155780
  415.7 5.5 %copy-start.5 = (bf16[1,896,2048]{2,1,0:T(8,128)(2,1)S(1)}, bf16[1,896,2048]{2,1,0:T(8,128)(2,1)}, u32[]{:S(2)}) copy-start(bf16[1,896,2048]{2,1,0:T(8,128)(2,1)} %param.13) | copy-start | bytes 11010052
  423.9 8.8 %copy-start.3 = (f32[64,8]{0,1:T(8,128)S(1)}, f32[64,8]{0,1:T(8,128)}, u32[]{:S(2)}) copy-start(f32[64,8]{0,1:T(8,128)} %param.12) | copy-start | bytes 6148
  425.2 28.0 %all-to-all-start.2 = ((bf16[32,18,896]{2,1,0:T(8,128)(2,1)}), bf16[32,18,896]{2,1,0:T(8,128)(2,1)S(1)}, u32[]{:S(2)}, u32[]{:S(2)}) async-start(bf16[32,18,896]{2,1,0:T(8,128)(2,1)} %reshape.81), calls=%async_computation.7 | async-start | bytes 2752512 | tf_op jit(solution)/shard_map/all_to_all | solution.py:71
Sparse Core Ops, SparseCore 0:
  49.3 59.1 reduce-scatter.11
  111.0 58.8 reduce-scatter.7
  172.5 58.8 reduce-scatter.9
  233.9 58.8 reduce-scatter.13
  295.2 58.8 reduce-scatter.5
  357.3 58.3 all-gather.1
where the time goes:
time: 464 us
  waiting for transfers between devices  308 us (66%)
  blocking collectives  68.4 us (15%)
  matrix products  39.8 us (9%)
  local copies, waits for them, and re-layouts  19.9 us (4%)
  between operations  13.6 us (3%)
  starting transfers between devices  7.92 us (2%)
  other arithmetic  6.42 us (1%)
    reduce_scatter x1, waiting for transfers between devices, shards(): lax.psum_scatter(part_tgate, 'dp', scatter_dimension=0, tiled=True)  61.5 us
    reduce_scatter x1, waiting for transfers between devices, shards(): lax.psum_scatter(part_tup, 'dp', scatter_dimension=0, tiled=True)  61.3 us
    reduce_scatter x1, waiting for transfers between devices, shards(): lax.psum_scatter(part_back, 'dp', scatter_dimension=0, tiled=True)  61.3 us
    all_gather x1, waiting for transfers between devices, shards(): piece = lax.all_gather(factors, 'dp', axis=1, tiled=True)  58.5 us
    reduce_scatter x1, waiting for transfers between devices, shards(): lax.psum_scatter(part_gate, 'dp', scatter_dimension=0, tiled=True)  44.6 us
    all_to_all x1, blocking collectives, shards(): lax.all_to_all(scatter_rows(paired), 'expert', split_axis=0, concat_axis=...  39.1 us
    all_to_all x1, blocking collectives, shards(): lax.all_to_all(scatter_rows(tokens), 'expert', split_axis=0, concat_axis=...  29.3 us
    all_to_all x1, waiting for transfers between devices, shards(): lax.all_to_all(outgoing, 'expert', split_axis=0, concat_axis=0, tiled=True)  20.4 us
  transfers between devices with their start and end apart: 7, of which 6 were waited for; matrix products, arithmetic and copies ran while one was open for 8% of the time, Pallas kernels for 0%

commit v1 on v0

--- a/solution.py
+++ b/solution.py
@@ -4,6 +4,24 @@
 from jax.sharding import PartitionSpec as P
 
 TOP = 8
+
+
+def ring_gather(shard, axis, dim):
+    ways, here, step = (lax.axis_size(axis), lax.axis_index(axis), shard.shape[dim])
+    shape = [n * ways if d == dim else n for d, n in enumerate(shard.shape)]
+    full = lax.dynamic_update_slice_in_dim(
+        jnp.zeros(shape, shard.dtype), shard, here * step, axis=dim
+    )
+    going_up = going_down = shard
+    for far in range(1, ways // 2 + 1):
+        going_up = lax.ppermute(going_up, axis, [(d, (d + 1) % ways) for d in range(ways)])
+        full = lax.dynamic_update_slice_in_dim(full, going_up, (here - far) % ways * step, axis=dim)
+        if 2 * far < ways:
+            going_down = lax.ppermute(going_down, axis, [(d, (d - 1) % ways) for d in range(ways)])
+            full = lax.dynamic_update_slice_in_dim(
+                full, going_down, (here + far) % ways * step, axis=dim
+            )
+    return full
 
 
 def second_order(pre_gate, pre_up, tangent_gate, tangent_up, back_hidden):
@@ -65,7 +83,7 @@
     )
     factor_a, factor_b = second_order(summed[0], summed[1], summed[2], summed[3], summed[4])
     factors = jnp.stack([factor_a, factor_b])
-    piece = lax.all_gather(factors, "dp", axis=1, tiled=True)
+    piece = ring_gather(factors, "dp", 1)
     result_rows = contract_last(piece[0], gate_cols) + contract_last(piece[1], up_cols)
     outgoing = result_rows.astype(jnp.bfloat16).reshape(expert_count, capacity, feat_cols)
     returned = lax.all_to_all(outgoing, "expert", split_axis=0, concat_axis=0, tiled=True).reshape(

time: 464 us -> 470 us (1.013)
  waiting for transfers between devices: 308 us -> 292 us
  starting transfers between devices: 7.92 us -> 19.5 us
  local copies, waits for them, and re-layouts: 19.9 us -> 28.6 us
    all_gather x1 -> x0, waiting for transfers between devices: 58.5 us -> none  [shards(): piece = lax.all_gather(factors, 'dp', axis=1, tiled=True)]
    ppermute x0 -> x7, waiting for transfers between devices: none -> 43.1 us  [the longest x4 43.1 us: ring_gather(): lax.ppermute(going_up, axis, [(d, (d + 1) % ways) for d in range(ways)])]
    ppermute x0 -> x7, starting transfers between devices: none -> 8 us  [the longest x3 7.99 us: ring_gather(): lax.ppermute(going_down, axis, [(d, (d - 1) % ways) for d in range(ways)])]
    dynamic_update_slice x0 -> x7, local copies, waits for them, and re-layouts: none -> 6.04 us  [the longest x4 3.43 us: ring_gather(): lax.dynamic_update_slice_in_dim(full, going_up, (here - far) % ways * ste...]
  transfers between devices with their start and end apart: 7 -> 13, of which waited for: 6 -> 9; matrix products, arithmetic and copies ran while one was open for 8% -> 9% of each run, Pallas kernels for 0% -> 0%
where the time goes in v1:
time: 470 us; the launch traced here: 469 us
  waiting for transfers between devices  292 us (62%)
  blocking collectives  68.4 us (15%)
  matrix products  40.4 us (9%)
  local copies, waits for them, and re-layouts  28.6 us (6%)
  starting transfers between devices  19.5 us (4%)
  between operations  13.3 us (3%)
  other arithmetic  6.52 us (1%)
    reduce_scatter x1, waiting for transfers between devices, shards(): lax.psum_scatter(part_back, 'dp', scatter_dimension=0, tiled=True)  61.5 us
    reduce_scatter x1, waiting for transfers between devices, shards(): lax.psum_scatter(part_tup, 'dp', scatter_dimension=0, tiled=True)  61.3 us
    reduce_scatter x1, waiting for transfers between devices, shards(): lax.psum_scatter(part_tgate, 'dp', scatter_dimension=0, tiled=True)  61.3 us
    reduce_scatter x1, waiting for transfers between devices, shards(): lax.psum_scatter(part_gate, 'dp', scatter_dimension=0, tiled=True)  44.6 us
    ppermute x4, waiting for transfers between devices, ring_gather(): lax.ppermute(going_up, axis, [(d, (d + 1) % ways) for d in range(ways)])  43.1 us
    all_to_all x1, blocking collectives, shards(): lax.all_to_all(scatter_rows(paired), 'expert', split_axis=0, concat_axis=...  39.1 us
    all_to_all x1, blocking collectives, shards(): lax.all_to_all(scatter_rows(tokens), 'expert', split_axis=0, concat_axis=...  29.3 us
    all_to_all x1, waiting for transfers between devices, shards(): lax.all_to_all(outgoing, 'expert', split_axis=0, concat_axis=0, tiled=True)  20.4 us
  transfers between devices with their start and end apart: 13, of which 9 were waited for; matrix products, arithmetic and copies ran while one was open for 9% of the time, Pallas kernels for 0%

profile of v1, /device:TPU:1, one launch (start us, length us, event | category | flops | bytes accessed | tf_op | source)
XLA Modules:
  0.0 469.1 jit_solution(16771063360271546530)
XLA Ops:
  10.0 3.0 scatter_custom_fusion.1
  13.3 29.3 %all_to_all.15 = bf16[32,18,896]{2,1,0:T(8,128)(2,1)S(1)} all-to-all(bf16[32,18,896]{2,1,0:T(8,128)(2,1)S(1)} %reshape.79), channel_id=1, replica_groups=mesh['dp'=8,'expert'=32] {'expert'}, dimensions={0} | all-to-all | bytes 2064384 | tf_op jit(solution)/shard_map/all_to_all | solution.py:60
  42.9 6.3 %fusion.4 = f32[576,2048]{1,0:T(8,128)} fusion(bf16[576,896]{1,0:T(8,128)(2,1)S(1)} %reshape.80, bf16[1,896,2048]{2,1,0:T(8,128)(2,1)} %param.14), kind=kOutput, calls=%fused_computation.7 | convolution fusion | flops 2113929216 | bytes 9420800 | tf_op jit(solution)/shard_map/dot_general | solution.py:73
  49.3 6.3 %fusion.10 = f32[576,2048]{1,0:T(8,128)} fusion(bf16[576,896]{1,0:T(8,128)(2,1)S(1)} %reshape.80, bf16[1,896,2048]{2,1,0:T(8,128)(2,1)} %param.13), kind=kOutput, calls=%fused_computation.13 | convolution fusion | flops 2113929216 | bytes 9420800 | tf_op jit(solution)/shard_map/dot_general | solution.py:72
  56.6 4.8 %scatter_custom_fusion = bf16[576,1792]{1,0:T(8,128)(2,1)} fusion(s32[512]{0:T(512)S(1)} %bitcast.64, bf16[]{:T(256)} %constant.62.clone.1, bf16[64,1792]{1,0:T(8,128)(2,1)S(1)} %pad_maximum_fusion.1), kind=kCustom, calls=%fused_computation.22 | custom fusion | bytes 2293762 | tf_op jit(solution)/shard_map/scatter | solution.py:58
  64.0 39.1 %all_to_all.16 = bf16[32,18,1792]{2,1,0:T(8,128)(2,1)} all-to-all(bf16[32,18,1792]{2,1,0:T(8,128)(2,1)S(1)} %reshape.76), channel_id=1, replica_groups=mesh['dp'=8,'expert'=32] {'expert'}, dimensions={0} | all-to-all | bytes 4128768 | tf_op jit(solution)/shard_map/all_to_all | solution.py:64
  103.1 2.8 reshape.77
  105.9 6.5 %fusion.12 = f32[576,2048]{1,0:T(8,128)} fusion(bf16[1,2048,896]{2,1,0:T(8,128)(2,1)} %param.15, bf16[576,1792]{1,0:T(8,128)(2,1)S(1)} %reshape.77), kind=kOutput, calls=%fused_computation.15 | convolution fusion | flops 2113929216 | bytes 9420800 | tf_op jit(solution)/shard_map/dot_general | solution.py:37
  112.7 6.3 %fusion.2 = f32[576,2048]{1,0:T(8,128)} fusion(bf16[1,896,2048]{2,1,0:T(8,128)(2,1)} %param.14, bf16[576,1792]{1,0:T(8,128)(2,1)S(1)} %reshape.77), kind=kOutput, calls=%fused_computation.5 | convolution fusion | flops 2113929216 | bytes 9420800 | tf_op jit(solution)/shard_map/dot_general | solution.py:75
  119.0 6.3 %fusion.8 = f32[576,2048]{1,0:T(8,128)} fusion(bf16[1,896,2048]{2,1,0:T(8,128)(2,1)} %param.13, bf16[576,1792]{1,0:T(8,128)(2,1)S(1)} %reshape.77), kind=kOutput, calls=%fused_computation.11 | convolution fusion | flops 2113929216 | bytes 9420800 | tf_op jit(solution)/shard_map/dot_general | solution.py:74
  125.4 44.6 %reduce-scatter.8.cloned.1.call-done = f32[72,2048]{1,0:T(8,128)} async-done(((f32[576,2048]{1,0:T(8,128)}), f32[72,2048]{1,0:T(8,128)}) %reduce-scatter.8.cloned.1.call-update) | async-done | bytes 589840 | tf_op jit(solution)/shard_map/reduce_scatter | solution.py:78
  169.9 61.5 %reduce-scatter.6.cloned.1.call-done = f32[72,2048]{1,0:T(8,128)} async-done(((f32[576,2048]{1,0:T(8,128)}), f32[72,2048]{1,0:T(8,128)}) %reduce-scatter.6.cloned.1.call-update) | async-done | bytes 589840 | tf_op jit(solution)/shard_map/reduce_scatter | solution.py:82
  231.4 61.3 %reduce-scatter.14.cloned.1.call-done = f32[72,2048]{1,0:T(8,128)} async-done(((f32[576,2048]{1,0:T(8,128)}), f32[72,2048]{1,0:T(8,128)}) %reduce-scatter.14.cloned.1.call-update) | async-done | bytes 589840 | tf_op jit(solution)/shard_map/reduce_scatter | solution.py:81
  292.8 61.3 %reduce-scatter.10.cloned.1.call-done = f32[72,2048]{1,0:T(8,128)} async-done(((f32[576,2048]{1,0:T(8,128)}), f32[72,2048]{1,0:T(8,128)}) %reduce-scatter.10.cloned.1.call-update) | async-done | bytes 589840 | tf_op jit(solution)/shard_map/reduce_scatter | solution.py:80
  356.3 2.7 broadcast_in_dim.20
  362.7 12.8 %collective-permute-done = bf16[2,72,2048]{2,1,0:T(8,128)(2,1)S(1)} collective-permute-done((bf16[2,72,2048]{2,1,0:T(8,128)(2,1)S(1)}, bf16[2,72,2048]{2,1,0:T(8,128)(2,1)S(1)}, u32[]{:S(2)}, u32[]{:S(2)}) %collective-permute-start) | collective-permute-done | bytes 589856 | tf_op jit(solution)/shard_map/ppermute | solution.py:17
  375.4 2.7 collective-permute-start.3
  378.1 11.9 %collective-permute-done.2 = bf16[2,72,2048]{2,1,0:T(8,128)(2,1)S(1)} collective-permute-done((bf16[2,72,2048]{2,1,0:T(8,128)(2,1)S(1)}, bf16[2,72,2048]{2,1,0:T(8,128)(2,1)S(1)}, u32[]{:S(2)}, u32[]{:S(2)}) %collective-permute-start.2) | collective-permute-done | bytes 589856 | tf_op jit(solution)/shard_map/ppermute | solution.py:17
  395.2 8.4 %collective-permute-done.4 = bf16[2,72,2048]{2,1,0:T(8,128)(2,1)S(1)} collective-permute-done((bf16[2,72,2048]{2,1,0:T(8,128)(2,1)S(1)}, bf16[2,72,2048]{2,1,0:T(8,128)(2,1)S(1)}, u32[]{:S(2)}, u32[]{:S(2)}) %collective-permute-start.4) | collective-permute-done | bytes 589856 | tf_op jit(solution)/shard_map/ppermute | solution.py:17
  406.2 10.1 %collective-permute-done.6 = bf16[2,72,2048]{2,1,0:T(8,128)(2,1)S(1)} collective-permute-done((bf16[2,72,2048]{2,1,0:T(8,128)(2,1)S(1)}, bf16[2,72,2048]{2,1,0:T(8,128)(2,1)S(1)}, u32[]{:S(2)}, u32[]{:S(2)}) %collective-permute-start.6) | collective-permute-done | bytes 589856 | tf_op jit(solution)/shard_map/ppermute | solution.py:17
  417.2 4.4 fusion
  421.6 4.3 add_convert_fusion
  427.2 11.1 %all-to-all-start.2 = ((bf16[32,18,896]{2,1,0:T(8,128)(2,1)}), bf16[32,18,896]{2,1,0:T(8,128)(2,1)S(1)}, u32[]{:S(2)}, u32[]{:S(2)}) async-start(bf16[32,18,896]{2,1,0:T(8,128)(2,1)} %reshape.81), calls=%async_computation.7 | async-start | bytes 2752512 | tf_op jit(solution)/shard_map/all_to_all | solution.py:89
  438.4 20.4 %all-to-all-done.2 = bf16[32,18,896]{2,1,0:T(8,128)(2,1)S(1)} async-done(((bf16[32,18,896]{2,1,0:T(8,128)(2,1)}), bf16[32,18,896]{2,1,0:T(8,128)(2,1)S(1)}, u32[]{:S(2)}, u32[]{:S(2)}) %all-to-all-start.2) | async-done | bytes 1032224 | tf_op jit(solution)/shard_map/all_to_all | solution.py:89
  (66 shorter events, 27.6 us)
Async XLA Ops:
  6.5 3.4 copy-start
  6.5 118.8 %reduce-scatter.12.cloned.1.call-start = ((), (), s32[]{:S(2)}) async-start(), calls=%async_computation.11 | async-start | bytes 5308416 | tf_op jit(solution)/shard_map/reduce_scatter | solution.py:79
  49.2 120.7 %reduce-scatter.8.cloned.1.call-start = ((), (), s32[]{:S(2)}) async-start(), calls=%async_computation.9 | async-start | bytes 5308416 | tf_op jit(solution)/shard_map/reduce_scatter | solution.py:78
  55.6 0.9 copy-start.2
  55.6 1.0 copy-start.3
  55.6 175.8 %reduce-scatter.6.cloned.1.call-start = ((), (), s32[]{:S(2)}) async-start(), calls=%async_computation.8 | async-start | bytes 5308416 | tf_op jit(solution)/shard_map/reduce_scatter | solution.py:82
  112.4 180.3 %reduce-scatter.14.cloned.1.call-start = ((), (), s32[]{:S(2)}) async-start(), calls=%async_computation.12 | async-start | bytes 5308416 | tf_op jit(solution)/shard_map/reduce_scatter | solution.py:81
  119.0 235.1 %reduce-scatter.10.cloned.1.call-start = ((), (), s32[]{:S(2)}) async-start(), calls=%async_computation.10 | async-start | bytes 5308416 | tf_op jit(solution)/shard_map/reduce_scatter | solution.py:80
  360.0 15.5 %collective-permute-start = (bf16[2,72,2048]{2,1,0:T(8,128)(2,1)S(1)}, bf16[2,72,2048]{2,1,0:T(8,128)(2,1)S(1)}, u32[]{:S(2)}, u32[]{:S(2)}) collective-permute-start(bf16[2,72,2048]{2,1,0:T(8,128)(2,1)S(1)} %get-tuple-element.7), channel_id=1, source_target_pairs={{0,32},{32,64},{64,96},{96,128},{128,160},{160,192},{192,224},{224... | collective-permute-start | bytes 1769480 | tf_op jit(solution)/shard_map/ppermute | solution.py:17
  360.0 15.5 %collective-permute-start.1 = (bf16[2,72,2048]{2,1,0:T(8,128)(2,1)S(1)}, bf16[2,72,2048]{2,1,0:T(8,128)(2,1)S(1)}, u32[]{:S(2)}, u32[]{:S(2)}) collective-permute-start(bf16[2,72,2048]{2,1,0:T(8,128)(2,1)S(1)} %get-tuple-element.7), channel_id=1, source_target_pairs={{0,224},{32,0},{64,32},{96,64},{128,96},{160,128},{192,160},{224,1... | collective-permute-start | bytes 1769480 | tf_op jit(solution)/shard_map/ppermute | solution.py:20
  375.4 14.5 %collective-permute-start.2 = (bf16[2,72,2048]{2,1,0:T(8,128)(2,1)S(1)}, bf16[2,72,2048]{2,1,0:T(8,128)(2,1)S(1)}, u32[]{:S(2)}, u32[]{:S(2)}) collective-permute-start(bf16[2,72,2048]{2,1,0:T(8,128)(2,1)S(1)} %collective-permute-done), channel_id=1, source_target_pairs={{0,32},{32,64},{64,96},{96,128},{128,160},{160,192},{192,224},{224... | collective-permute-start | bytes 1769480 | tf_op jit(solution)/shard_map/ppermute | solution.py:17
  375.4 16.3 %collective-permute-start.3 = (bf16[2,72,2048]{2,1,0:T(8,128)(2,1)S(1)}, bf16[2,72,2048]{2,1,0:T(8,128)(2,1)S(1)}, u32[]{:S(2)}, u32[]{:S(2)}) collective-permute-start(bf16[2,72,2048]{2,1,0:T(8,128)(2,1)S(1)} %collective-permute-done.1), channel_id=1, source_target_pairs={{0,224},{32,0},{64,32},{96,64},{128,96},{160,128},{192,160},{224,1... | collective-permute-start | bytes 1769480 | tf_op jit(solution)/shard_map/ppermute | solution.py:20
  390.0 13.6 %collective-permute-start.4 = (bf16[2,72,2048]{2,1,0:T(8,128)(2,1)S(1)}, bf16[2,72,2048]{2,1,0:T(8,128)(2,1)S(1)}, u32[]{:S(2)}, u32[]{:S(2)}) collective-permute-start(bf16[2,72,2048]{2,1,0:T(8,128)(2,1)S(1)} %collective-permute-done.2), channel_id=1, source_target_pairs={{0,32},{32,64},{64,96},{96,128},{128,160},{160,192},{192,224},{224... | collective-permute-start | bytes 1769480 | tf_op jit(solution)/shard_map/ppermute | solution.py:17
  390.8 26.3 %copy-start.5 = (bf16[1,896,2048]{2,1,0:T(8,128)(2,1)S(1)}, bf16[1,896,2048]{2,1,0:T(8,128)(2,1)}, u32[]{:S(2)}) copy-start(bf16[1,896,2048]{2,1,0:T(8,128)(2,1)} %param.14) | copy-start | bytes 11010052
  391.7 13.6 %collective-permute-start.5 = (bf16[2,72,2048]{2,1,0:T(8,128)(2,1)S(1)}, bf16[2,72,2048]{2,1,0:T(8,128)(2,1)S(1)}, u32[]{:S(2)}, u32[]{:S(2)}) collective-permute-start(bf16[2,72,2048]{2,1,0:T(8,128)(2,1)S(1)} %collective-permute-done.3), channel_id=1, source_target_pairs={{0,224},{32,0},{64,32},{96,64},{128,96},{160,128},{192,160},{224,1... | collective-permute-start | bytes 1769480 | tf_op jit(solution)/shard_map/ppermute | solution.py:20
  403.6 12.7 %collective-permute-start.6 = (bf16[2,72,2048]{2,1,0:T(8,128)(2,1)S(1)}, bf16[2,72,2048]{2,1,0:T(8,128)(2,1)S(1)}, u32[]{:S(2)}, u32[]{:S(2)}) collective-permute-start(bf16[2,72,2048]{2,1,0:T(8,128)(2,1)S(1)} %collective-permute-done.4), channel_id=1, source_target_pairs={{0,32},{32,64},{64,96},{96,128},{128,160},{160,192},{192,224},{224... | collective-permute-start | bytes 1769480 | tf_op jit(solution)/shard_map/ppermute | solution.py:17
  417.2 4.5 copy-start.6
  425.9 12.4 %copy-start.4 = (f32[64,8]{0,1:T(8,128)S(1)}, f32[64,8]{0,1:T(8,128)}, u32[]{:S(2)}) copy-start(f32[64,8]{0,1:T(8,128)} %param.12) | copy-start | bytes 6148
  427.2 31.6 %all-to-all-start.2 = ((bf16[32,18,896]{2,1,0:T(8,128)(2,1)}), bf16[32,18,896]{2,1,0:T(8,128)(2,1)S(1)}, u32[]{:S(2)}, u32[]{:S(2)}) async-start(bf16[32,18,896]{2,1,0:T(8,128)(2,1)} %reshape.81), calls=%async_computation.7 | async-start | bytes 2752512 | tf_op jit(solution)/shard_map/all_to_all | solution.py:89
  458.8 3.7 copy-start.1
Sparse Core Ops, SparseCore 0:
  49.3 59.1 reduce-scatter.11
  111.0 58.8 reduce-scatter.7
  172.5 58.8 reduce-scatter.5
  233.8 58.8 reduce-scatter.13
  295.2 58.8 reduce-scatter.9
